TPU v7x, 768 devices: a whole 4x8x12 slice. The times are simulated.
768 devices in a mesh: replica: 96 (over y_hi, z, core), fsdp: 8 (over x, y_lo).
Axes of the slice: x: 4, y: 8 (y_hi: 4, y_lo: 2; y = y_hi * 2 + y_lo), z: 12, core: 2. Of those that a mesh axis runs over, the one named last changes fastest.
Arguments:
- local_params: float32 [96, 48, 8192], P('replica', 'fsdp'), may hold values from -6 to 6
- global_params: float32 [48, 8192], P('fsdp'), may hold values from -6 to 6
- momentum: float32 [48, 8192], P('fsdp'), may hold values from -6 to 6
- layer_input: bfloat16 [96, 1024, 512], P('replica', 'fsdp'), may hold values from -6 to 6
- output_grad: bfloat16 [96, 1024, 8192], P('replica', 'fsdp'), may hold values from -0.1875 to 0.1875
- token_ids: int32 [96, 1024], P('replica', 'fsdp'), may hold values from 0 to 65023, as said below
Outputs:
- new_global: float32 [48, 8192], P('fsdp')
- new_momentum: float32 [48, 8192], P('fsdp')
- inner_grad: bfloat16 [96, 512, 8192], P('replica', 'fsdp')
Inputs may be any that keep to these rules, and one draw needn't show every extreme that they name: `token_ids`: id 0 is padding; it fills a tail of 1 to 256 positions of each of a replica's 2 sequences, and no other position.
All inputs are finite; a program needn't handle non-finite values.
Results may differ from a plain program's by a relative error of at most 0.017.
Values may be sent and summed in bfloat16 or wider, within the bound.
A program may use at most 64 MiB of HBM per device.

v0:
```python
import jax
import jax.numpy as jnp
from jax import lax
from jax.sharding import PartitionSpec as P

EPS = 1e-06
MU = 0.9
LR = 0.7


def outer_update(average, global_part, momentum_part):
    fresh = MU * momentum_part + average
    return (global_part - LR * (average + MU * fresh), fresh)


def local(local_params, global_params, momentum, layer_input, output_grad, token_ids):
    shape = global_params.shape
    delta = global_params - local_params[0]
    blocks = delta.reshape(-1, 128)
    scale = (jnp.max(jnp.abs(blocks), axis=1, keepdims=True) + EPS).astype(jnp.bfloat16)
    scale_wide = scale.astype(jnp.float32)
    codes = (blocks / scale_wide).astype(jnp.bfloat16)
    global_blocks = global_params.reshape(-1, 128)
    momentum_blocks = momentum.reshape(-1, 128)
    count = lax.axis_size("replica")
    values = codes.astype(jnp.float32) * scale_wide
    average = lax.psum(values, "replica") / count
    new_global, new_momentum = outer_update(average, global_blocks, momentum_blocks)
    keep = (token_ids[0] != 0)[:, None]
    masked = jnp.where(keep, output_grad[0], jnp.zeros((), jnp.bfloat16))
    inputs = layer_input[0]
    grad_rows = lax.psum_scatter(
        lax.dot_general(
            inputs, masked, (((0,), (0,)), ((), ())), preferred_element_type=jnp.float32
        ).astype(jnp.bfloat16),
        "fsdp",
        scatter_dimension=0,
        tiled=True,
    )
    inner_grad = grad_rows[None]
    return (new_global.reshape(shape), new_momentum.reshape(shape), inner_grad)


def solution(mesh):
    return jax.shard_map(
        local,
        mesh=mesh,
        in_specs=(
            P("replica", "fsdp", None),
            P("fsdp", None),
            P("fsdp", None),
            P("replica", "fsdp", None),
            P("replica", "fsdp", None),
            P("replica", "fsdp"),
        ),
        out_specs=(P("fsdp", None), P("fsdp", None), P("replica", "fsdp", None)),
        check_vma=False,
    )
```

profile of v0, /device:TPU:1, one launch (start us, length us, event | category | flops | bytes accessed | tf_op | source)
XLA Modules:
  0.0 762.5 jit_solution(1493634854577224920)
XLA Ops:
  8.0 0.0 copy-start
  8.0 0.0 all-reduce.2.cloned.1.call-start
  8.1 1.2 bitcast_subtract_fusion
  9.2 0.1 reshape.45
  9.3 0.1 abs_reduce_fusion
  9.5 0.8 convert_multiply_fusion
  10.3 0.0 all-reduce.2.cloned.1.call-update
  10.3 0.0 reduce-scatter.4.cloned.1.call-start
  10.4 0.7 compare_bitcast_fusion
  11.0 0.0 copy-done
  11.0 7.3 fusion
  18.3 11.6 %copy.11 = bf16[512,8192]{1,0:T(8,128)(2,1)} copy(bf16[512,8192]{0,1:T(8,128)(2,1)} %fusion) | data formatting | bytes 16777216
  29.9 0.0 copy-start.1
  29.9 0.0 copy-start.2
  29.9 0.0 reduce-scatter.4.cloned.1.call-update
  29.9 0.9 copy-done.1
  30.8 0.1 reshape.44
  30.9 0.0 copy-done.2
  31.0 0.1 mul.23
  31.1 717.8 %all-reduce.2.cloned.1.call-done = f32[384,128]{1,0:T(8,128)} async-done(((f32[384,128]{1,0:T(8,128)}), f32[384,128]{1,0:T(8,128)}) %all-reduce.2.cloned.1.call-update) | async-done | bytes 196624 | tf_op jit(solution)/shard_map/psum | solution.py:27
  748.9 1.0 multiply_add_fusion
  749.9 0.7 reshape.47
  750.6 0.7 reshape.46
  751.4 0.0 reduce-scatter.4.cloned.1.call-done
  751.4 2.0 copy.12
  753.4 1.6 copy.10
  (2 shorter events, 0.0 us)
Async XLA Ops:
  8.0 3.0 copy-start
  8.0 740.9 %all-reduce.2.cloned.1.call-start = ((), (), s32[]{:S(2)}) async-start(), calls=%async_computation.1 | async-start | bytes 393216 | tf_op jit(solution)/shard_map/psum | solution.py:27
  10.3 741.1 %reduce-scatter.4.cloned.1.call-start = ((), (), s32[]{:S(2)}) async-start(), calls=%async_computation.2 | async-start | bytes 9437184
  29.9 0.9 copy-start.1
  29.9 1.1 copy-start.2
Sparse Core Ops, SparseCore 0:
  12.6 736.2 all-reduce.1
Sparse Core Ops, SparseCore 1:
  30.0 184.6 reduce-scatter.3
where the time goes:
time: 766 us; the launch traced here: 762 us
  waiting for transfers between devices  718 us (94%)
  local copies, waits for them, and re-layouts  17.9 us (2%)
  between operations  15.5 us (2%)
    psum x1, waiting for transfers between devices, local(): average = lax.psum(values, 'replica') / count  718 us
    unnamed x9, local copies, waits for them, and re-layouts  16.1 us
  transfers between devices with their start and end apart: 2, of which 1 were waited for; matrix products, arithmetic and copies ran while one was open for 3% of the time, Pallas kernels for 0%

commit v1 on v0

v1 whole, which is shorter than its diff:
```python
import functools

import jax
import jax.numpy as jnp
from jax import lax
from jax.experimental import pallas as pl
from jax.experimental.pallas import tpu as pltpu
from jax.sharding import PartitionSpec as P

EPS = 1e-06
MU = 0.9
LR = 0.7
MESH = pl.DeviceIdType.MESH

BLOCK = 128
NX = 4
NY = 2
CHUNKS = 8


def ds(start, size):
    return pl.ds(pl.multiple_of(start, size), size)


def kernel(
    dims,
    local_hbm, global_hbm, momentum_hbm, input_hbm, grad_hbm, ids_hbm,
    new_global_ref, new_momentum_ref, out_ref,
    local_v, global_v, momentum_v, input_v, ids_v,
    global_rows, values, part1, part2, average,
    inputs_t, grads, y_out, y_in, own_half, done,
    load_sem, own_sem, store_sem,
    l_send, l_recv, g_send, g_recv, y_send, y_recv, o_send, o_recv,
    a1_send, a1_recv, a2_send, a2_recv, a3_send, a3_recv,
):
    NYH, NZ, NC = dims
    replica, me = lax.axis_index("replica"), lax.axis_index("fsdp")
    x, y = lax.div(me, NY), lax.rem(me, NY)
    core = lax.rem(replica, NC)
    z = lax.rem(lax.div(replica, NC), NZ)
    yh = lax.div(replica, NC * NZ)

    tokens, d = grad_hbm.shape
    r_in = input_v.shape[1]
    rows = r_in // (NX * NY)
    half = r_in // NY
    cols = d // NX
    w = cols // CHUNKS
    n_blocks = d // BLOCK
    frag = global_v.shape[0]
    n_rows = local_v.shape[0]
    rz = n_rows // NZ

    def x_peer(dx):
        px = lax.rem(x + dx, NX)
        return px, (replica, px * NY + y)

    y_peer = (replica, x * NY + (1 - y))

    def z_peer(dz):
        pz = lax.rem(z + dz, NZ)
        return pz, ((yh * NZ + pz) * NC + core, me)

    group = NYH * NC
    g_me = yh * NC + core

    def g_peer(k):
        pk = lax.rem(g_me + k, group)
        return pk, ((lax.div(pk, NC) * NZ + z) * NC + lax.rem(pk, NC), me)

    loads = [
        pltpu.make_async_copy(src, dst, load_sem.at[i])
        for i, (src, dst) in enumerate(
            [(input_hbm, input_v), (ids_hbm, ids_v), (global_hbm, global_v), (local_hbm, local_v), (momentum_hbm, momentum_v)]
        )
    ]
    for copy in loads:
        copy.start()
    own_grads = pltpu.make_async_copy(
        grad_hbm.at[:, ds(x * cols, cols)], grads.at[ds(x * tokens, tokens), :], own_sem
    )
    own_grads.start()

    barrier = pltpu.get_barrier_semaphore()
    peers = [x_peer(dx)[1] for dx in range(1, NX)] + [y_peer]
    peers += [z_peer(dz)[1] for dz in range(1, NZ)]
    peers += [g_peer(k)[1] for k in range(1, group)]
    for peer in peers:
        pl.semaphore_signal(barrier, inc=1, device_id=peer, device_id_type=MESH)

    loads[0].wait()
    loads[1].wait()
    turned = jnp.transpose(input_v[...].astype(jnp.float32))
    turned = jnp.where(ids_v[...] != 0, turned, 0.0).astype(jnp.bfloat16)
    for py in range(NY):
        for px in range(NX):
            block = (px * NY + py) * rows
            inputs_t[py, px * rows : (px + 1) * rows, ds(x * tokens, tokens)] = turned[block : block + rows, :]

    loads[2].wait()
    for j in range(n_blocks):
        global_rows[:, j, :] = global_v[:, j * BLOCK : (j + 1) * BLOCK]
    loads[3].wait()
    delta = global_rows[...].reshape(n_rows, BLOCK) - local_v[...]
    scale = (jnp.max(jnp.abs(delta), axis=1, keepdims=True) + EPS).astype(jnp.bfloat16).astype(jnp.float32)
    codes = (delta / scale).astype(jnp.bfloat16)
    values[...] = (codes.astype(jnp.float32) * scale).astype(jnp.bfloat16)

    pl.semaphore_wait(barrier, len(peers))

    sends = []

    def send(src, dst, send_sem, recv_sem, device):
        copy = pltpu.make_async_remote_copy(
            src_ref=src, dst_ref=dst, send_sem=send_sem, recv_sem=recv_sem, device_id=device, device_id_type=MESH
        )
        copy.start()
        sends.append(copy)
        return copy

    a1 = []
    for dz in range(1, NZ):
        pz, device = z_peer(dz)
        a1.append(send(values.at[ds(pz * rz, rz), :], part1.at[z], a1_send.at[dz], a1_recv.at[dz], device))
    ls = []
    for dx in range(1, NX):
        px, device = x_peer(dx)
        mine = inputs_t.at[:, :, ds(x * tokens, tokens)]
        ls.append(send(mine, mine, l_send.at[dx], l_recv.at[dx], device))

    gs = [[] for _ in range(CHUNKS)]

    def send_grads(c):
        for dx in range(1, NX):
            px, device = x_peer(dx)
            gs[c].append(
                send(
                    grad_hbm.at[:, ds(px * cols + c * w, w)],
                    grads.at[ds(x * tokens, tokens), c * w : (c + 1) * w],
                    g_send.at[c, dx], g_recv.at[c, dx], device,
                )
            )

    for c in range(CHUNKS):
        send_grads(c)

    def reduce_z():
        part1[z] = values[ds(z * rz, rz), :]
        for copy in a1:
            copy.wait_recv()
        part2[g_me] = jnp.sum(part1[...].astype(jnp.float32), axis=0)
        return [
            send(part2.at[g_me], part2.at[g_me], a2_send.at[k], a2_recv.at[k], g_peer(k)[1]) for k in range(1, group)
        ]

    def reduce_group(a2):
        for copy in a2:
            copy.wait_recv()
        mine = average.at[ds(z * rz, rz), :]
        mine[...] = jnp.sum(part2[...], axis=0) / float(NZ * group)
        return [send(mine, mine, a3_send.at[dz], a3_recv.at[dz], z_peer(dz)[1]) for dz in range(1, NZ)]

    def outer_update(a3):
        for copy in a3:
            copy.wait_recv()
        loads[4].wait()
        global_rows[...] = average[...].reshape(frag, n_blocks, BLOCK)
        for j in range(n_blocks):
            at = slice(j * BLOCK, (j + 1) * BLOCK)
            mean = global_rows[:, j, :]
            fresh = MU * momentum_v[:, at] + mean
            new_momentum_ref[:, at] = fresh
            new_global_ref[:, at] = global_v[:, at] - LR * (mean + MU * fresh)

    ys, outs = [], []

    def multiply(c):
        at = slice(c * w, (c + 1) * w)
        if c == 0:
            own_grads.wait()
            for copy in ls:
                copy.wait_recv()
        for copy in gs[c]:
            copy.wait_recv()
        block = grads[:, at]
        y_out[c] = jnp.dot(inputs_t[1 - y], block, preferred_element_type=jnp.float32).astype(jnp.bfloat16)
        ys.append(send(y_out.at[c], y_in.at[c], y_send.at[c], y_recv.at[c], y_peer))
        own_half[c % 2] = jnp.dot(inputs_t[y], block, preferred_element_type=jnp.float32)

    stores = []

    def finish(c):
        ys[c].wait_recv()
        done[c] = (own_half[c % 2] + y_in[c].astype(jnp.float32)).astype(jnp.bfloat16)
        to = ds(x * cols + c * w, w)
        for dx in range(1, NX):
            px, device = x_peer(dx)
            outs.append(send(done.at[c, ds(px * rows, rows), :], out_ref.at[:, to], o_send.at[c, dx], o_recv.at[c, dx], device))
        store = pltpu.make_async_copy(done.at[c, ds(x * rows, rows), :], out_ref.at[:, to], store_sem.at[c])
        store.start()
        stores.append(store)

    a2 = reduce_z()
    a3 = None
    for c in range(CHUNKS):
        multiply(c)
        if c == 0:
            a3 = reduce_group(a2)
        else:
            finish(c - 1)
    outer_update(a3)
    finish(CHUNKS - 1)

    for copy in outs:
        copy.wait_recv()
    for copy in stores:
        copy.wait()
    for copy in sends:
        copy.wait_send()


def local(dims, local_params, global_params, momentum, layer_input, output_grad, token_ids):
    frag, d = global_params.shape
    tokens, r_in = layer_input.shape[1:]
    n_rows = frag * d // BLOCK
    nz, group = dims[1], dims[0] * dims[2]
    half, cols, rows = r_in // NY, d // NX, r_in // (NX * NY)
    w = cols // CHUNKS
    f32, bf16 = jnp.float32, jnp.bfloat16
    dma = pltpu.SemaphoreType.DMA
    anywhere = pl.BlockSpec(memory_space=pl.ANY)
    vmem = pl.BlockSpec(memory_space=pltpu.VMEM)
    new_global, new_momentum, inner_grad = pl.pallas_call(
        functools.partial(kernel, dims),
        out_shape=(
            jax.ShapeDtypeStruct((frag, d), f32),
            jax.ShapeDtypeStruct((frag, d), f32),
            jax.ShapeDtypeStruct((rows, d), bf16),
        ),
        in_specs=[anywhere] * 6,
        out_specs=(vmem, vmem, anywhere),
        scratch_shapes=[
            pltpu.VMEM((n_rows, BLOCK), f32),
            pltpu.VMEM((frag, d), f32),
            pltpu.VMEM((frag, d), f32),
            pltpu.VMEM((tokens, r_in), bf16),
            pltpu.VMEM((1, tokens), jnp.int32),
            pltpu.VMEM((frag, d // BLOCK, BLOCK), f32),
            pltpu.VMEM((n_rows, BLOCK), bf16),
            pltpu.VMEM((nz, n_rows // nz, BLOCK), bf16),
            pltpu.VMEM((group, n_rows // nz, BLOCK), f32),
            pltpu.VMEM((n_rows, BLOCK), f32),
            pltpu.VMEM((NY, half, NX * tokens), bf16),
            pltpu.VMEM((NX * tokens, cols), bf16),
            pltpu.VMEM((CHUNKS, half, w), bf16),
            pltpu.VMEM((CHUNKS, half, w), bf16),
            pltpu.VMEM((2, half, w), f32),
            pltpu.VMEM((CHUNKS, half, w), bf16),
            dma((5,)), dma(()), dma((CHUNKS,)),
            dma((NX,)), dma((NX,)),
            dma((CHUNKS, NX)), dma((CHUNKS, NX)),
            dma((CHUNKS,)), dma((CHUNKS,)),
            dma((CHUNKS, NX)), dma((CHUNKS, NX)),
            dma((nz,)), dma((nz,)),
            dma((group,)), dma((group,)),
            dma((nz,)), dma((nz,)),
        ],
        compiler_params=pltpu.CompilerParams(
            collective_id=0, has_side_effects=True, vmem_limit_bytes=32 * 1024 * 1024
        ),
    )(
        local_params.reshape(n_rows, BLOCK),
        global_params,
        momentum,
        layer_input[0],
        output_grad[0],
        token_ids,
    )
    return new_global, new_momentum, inner_grad[None]


def build(mesh, dims):
    return jax.shard_map(
        functools.partial(local, dims),
        mesh=mesh,
        in_specs=(
            P("replica", "fsdp", None),
            P("fsdp", None),
            P("fsdp", None),
            P("replica", "fsdp", None),
            P("replica", "fsdp", None),
            P("replica", "fsdp"),
        ),
        out_specs=(P("fsdp", None), P("fsdp", None), P("replica", "fsdp", None)),
        check_vma=False,
    )


def solution(mesh):
    return build(mesh, (4, 12, 2))
```

time: 766 us -> 70 us (0.09)
  waiting for transfers between devices: 718 us -> 0 us
  Pallas kernels: 0 us -> 60.3 us
  between operations: 15.5 us -> 0.65 us
  local copies, waits for them, and re-layouts: 17.9 us -> 8.34 us
    psum x1 -> x0, waiting for transfers between devices: 718 us -> none  [local(): average = lax.psum(values, 'replica') / count]
    pallas_call x0 -> x1, Pallas kernels: none -> 60.3 us  [local(): pl.pallas_call(functools.partial(kernel, dims), out_shape=(jax.ShapeDtype...]
    unnamed x9 -> x15, local copies, waits for them, and re-layouts: 16.1 us -> 8.34 us
  transfers between devices with their start and end apart: 2 -> 0, of which waited for: 1 -> 0; matrix products, arithmetic and copies ran while one was open for 3% -> 0% of each run, Pallas kernels for 0% -> 0%
where the time goes in v1:
time: 70 us; the launch traced here: 69.3 us
  Pallas kernels  60.3 us (86%)
  local copies, waits for them, and re-layouts  8.34 us (12%)
    pallas_call x1, Pallas kernels, local(): pl.pallas_call(functools.partial(kernel, dims), out_shape=(jax.ShapeDtype...  60.3 us
    unnamed x15, local copies, waits for them, and re-layouts  8.34 us

profile of v1, /device:TPU:1, one launch (start us, length us, event | category | flops | bytes accessed | tf_op | source)
XLA Modules:
  0.0 69.3 jit_solution(12627259367498703886)
XLA Ops:
  0.6 0.0 copy-start
  0.6 1.6 %copy-done = bf16[1,128,8192]{2,1,0:T(8,128)(2,1)S(1)} copy-done((bf16[1,128,8192]{2,1,0:T(8,128)(2,1)S(1)}, bf16[1,128,8192]{2,1,0:T(8,128)(2,1)}, u32[]{:S(2)}) %copy-start) | copy-done | bytes 2097176
  2.2 0.0 copy-start.1
  2.2 0.9 %copy-done.1 = f32[6,8192]{1,0:T(8,128)S(1)} copy-done((f32[6,8192]{1,0:T(8,128)S(1)}, f32[6,8192]{1,0:T(8,128)}, u32[]{:S(2)}) %copy-start.1) | copy-done | bytes 196632
  3.2 0.0 copy-start.2
  3.2 0.9 %copy-done.2 = f32[6,8192]{1,0:T(8,128)S(1)} copy-done((f32[6,8192]{1,0:T(8,128)S(1)}, f32[6,8192]{1,0:T(8,128)}, u32[]{:S(2)}) %copy-start.2) | copy-done | bytes 196632
  4.1 0.0 copy-start.3
  4.1 0.9 %copy-done.3 = f32[1,6,8192]{2,0,1:T(1,128)S(1)} copy-done((f32[1,6,8192]{2,0,1:T(1,128)S(1)}, f32[1,6,8192]{2,0,1:T(1,128)}, u32[]{:S(2)}) %copy-start.3) | copy-done | bytes 196632
  5.1 0.0 copy-start.4
  5.1 0.9 %copy-done.4 = bf16[1,128,512]{2,1,0:T(8,128)(2,1)S(1)} copy-done((bf16[1,128,512]{2,1,0:T(8,128)(2,1)S(1)}, bf16[1,128,512]{2,1,0:T(8,128)(2,1)}, u32[]{:S(2)}) %copy-start.4) | copy-done | bytes 131096
  6.0 0.0 copy-start.5
  6.0 0.7 copy-done.5
  6.6 60.3 %shard_map.85 = (f32[6,8192]{1,0:T(8,128)S(1)}, f32[6,8192]{1,0:T(8,128)S(1)}, bf16[64,8192]{1,0:T(8,128)(2,1)S(1)}) custom-call(f32[384,128]{1,0:T(8,128)S(1)} %bitcast.6, f32[6,8192]{1,0:T(8,128)S(1)} %copy-done.1, f32[6,8192]{1,0:T(8,128)S(1)} %copy-done.2, bf16[128,512]{1,0:T(8,128)(2,1)S(1)} %bitcast.7, bf16[128,8192]{1,0:T(8,128)(2,1)S(1)} %bitcast.4, ...), custom_call_target="tpu_custom_call" | custom-call | tf_op jit(solution)/shard_map/pallas_call | solution.py:233
  66.9 0.7 %copy.12 = f32[6,8192]{1,0:T(8,128)} copy(f32[6,8192]{1,0:T(8,128)S(1)} %get-tuple-element.12) | data formatting | bytes 393216
  67.6 0.7 %copy.13 = f32[6,8192]{1,0:T(8,128)} copy(f32[6,8192]{1,0:T(8,128)S(1)} %get-tuple-element.13) | data formatting | bytes 393216
  68.3 1.0 %copy.14 = bf16[1,64,8192]{2,1,0:T(8,128)(2,1)} copy(bf16[1,64,8192]{2,1,0:T(8,128)(2,1)S(1)} %bitcast.5) | data formatting | bytes 2097152
Async XLA Ops:
  0.6 1.6 %copy-start = (bf16[1,128,8192]{2,1,0:T(8,128)(2,1)S(1)}, bf16[1,128,8192]{2,1,0:T(8,128)(2,1)}, u32[]{:S(2)}) copy-start(bf16[1,128,8192]{2,1,0:T(8,128)(2,1)} %param.10) | copy-start | bytes 6291460
  2.2 0.9 %copy-start.1 = (f32[6,8192]{1,0:T(8,128)S(1)}, f32[6,8192]{1,0:T(8,128)}, u32[]{:S(2)}) copy-start(f32[6,8192]{1,0:T(8,128)} %global_hbm.1) | copy-start | bytes 589828
  3.2 0.9 %copy-start.2 = (f32[6,8192]{1,0:T(8,128)S(1)}, f32[6,8192]{1,0:T(8,128)}, u32[]{:S(2)}) copy-start(f32[6,8192]{1,0:T(8,128)} %momentum_hbm.1) | copy-start | bytes 589828
  4.1 0.9 %copy-start.3 = (f32[1,6,8192]{2,0,1:T(1,128)S(1)}, f32[1,6,8192]{2,0,1:T(1,128)}, u32[]{:S(2)}) copy-start(f32[1,6,8192]{2,0,1:T(1,128)} %param.6) | copy-start | bytes 589828
  5.1 0.9 %copy-start.4 = (bf16[1,128,512]{2,1,0:T(8,128)(2,1)S(1)}, bf16[1,128,512]{2,1,0:T(8,128)(2,1)}, u32[]{:S(2)}) copy-start(bf16[1,128,512]{2,1,0:T(8,128)(2,1)} %param.9) | copy-start | bytes 393220
  6.0 0.7 copy-start.5

commit v2 on v1

--- a/solution.py
+++ b/solution.py
@@ -16,6 +16,10 @@
 NX = 4
 NY = 2
 CHUNKS = 8
+INIT = 1
+WAYS = (2, 1, 3)
+EARLY_Z = 5
+EARLY_STEPS, LATE_STEPS = (1, 3, 4), (0, 1, 2)
 
 
 def ds(start, size):
@@ -30,6 +34,7 @@
     global_rows, values, part1, part2, average,
     inputs_t, grads, y_out, y_in, own_half, done,
     load_sem, own_sem, store_sem,
+    go_sem, far_sem,
     l_send, l_recv, g_send, g_recv, y_send, y_recv, o_send, o_recv,
     a1_send, a1_recv, a2_send, a2_recv, a3_send, a3_recv,
 ):
@@ -82,51 +87,37 @@
     own_grads.start()
 
     barrier = pltpu.get_barrier_semaphore()
-    peers = [x_peer(dx)[1] for dx in range(1, NX)] + [y_peer]
-    peers += [z_peer(dz)[1] for dz in range(1, NZ)]
-    peers += [g_peer(k)[1] for k in range(1, group)]
-    for peer in peers:
-        pl.semaphore_signal(barrier, inc=1, device_id=peer, device_id_type=MESH)
-
-    loads[0].wait()
-    loads[1].wait()
-    turned = jnp.transpose(input_v[...].astype(jnp.float32))
-    turned = jnp.where(ids_v[...] != 0, turned, 0.0).astype(jnp.bfloat16)
-    for py in range(NY):
-        for px in range(NX):
-            block = (px * NY + py) * rows
-            inputs_t[py, px * rows : (px + 1) * rows, ds(x * tokens, tokens)] = turned[block : block + rows, :]
-
-    loads[2].wait()
-    for j in range(n_blocks):
-        global_rows[:, j, :] = global_v[:, j * BLOCK : (j + 1) * BLOCK]
-    loads[3].wait()
-    delta = global_rows[...].reshape(n_rows, BLOCK) - local_v[...]
-    scale = (jnp.max(jnp.abs(delta), axis=1, keepdims=True) + EPS).astype(jnp.bfloat16).astype(jnp.float32)
-    codes = (delta / scale).astype(jnp.bfloat16)
-    values[...] = (codes.astype(jnp.float32) * scale).astype(jnp.bfloat16)
-
-    pl.semaphore_wait(barrier, len(peers))
+    first, second = replica - core, replica - core + 1
+    near = [lax.rem(x + dx, NX) * NY + y for dx in range(1, NX)] + [x * NY + (1 - y)]
+    for peer in near:
+        pl.semaphore_signal(barrier, inc=1, device_id=(first, peer), device_id_type=MESH)
+
+    @pl.when(core == 1)
+    def _():
+        pl.semaphore_signal(barrier, inc=1, device_id=(first, me), device_id_type=MESH)
+
+    @pl.when(core == 0)
+    def _():
+        pl.semaphore_wait(barrier, NC * len(near) + 1)
+        pl.semaphore_signal(go_sem, inc=1, device_id=(second, me), device_id_type=MESH)
+
+    @pl.when(core == 1)
+    def _():
+        pl.semaphore_wait(go_sem, 1)
 
     sends = []
 
-    def send(src, dst, send_sem, recv_sem, device):
+    def remote(src, dst, send_sem, recv_sem, device):
         copy = pltpu.make_async_remote_copy(
             src_ref=src, dst_ref=dst, send_sem=send_sem, recv_sem=recv_sem, device_id=device, device_id_type=MESH
         )
-        copy.start()
         sends.append(copy)
         return copy
 
-    a1 = []
-    for dz in range(1, NZ):
-        pz, device = z_peer(dz)
-        a1.append(send(values.at[ds(pz * rz, rz), :], part1.at[z], a1_send.at[dz], a1_recv.at[dz], device))
-    ls = []
-    for dx in range(1, NX):
-        px, device = x_peer(dx)
-        mine = inputs_t.at[:, :, ds(x * tokens, tokens)]
-        ls.append(send(mine, mine, l_send.at[dx], l_recv.at[dx], device))
+    def send(*operands):
+        copy = remote(*operands)
+        copy.start()
+        return copy
 
     gs = [[] for _ in range(CHUNKS)]
 
@@ -141,26 +132,78 @@
                 )
             )
 
-    for c in range(CHUNKS):
+    for c in range(INIT):
         send_grads(c)
+
+    loads[0].wait()
+    loads[1].wait()
+    turned = jnp.transpose(input_v[...].astype(jnp.float32))
+    turned = jnp.where(ids_v[...] != 0, turned, 0.0).astype(jnp.bfloat16)
+    for py in range(NY):
+        for px in range(NX):
+            block = (px * NY + py) * rows
+            inputs_t[py, px * rows : (px + 1) * rows, ds(x * tokens, tokens)] = turned[block : block + rows, :]
+
+    mine = inputs_t.at[:, :, ds(x * tokens, tokens)]
+    ls = [send(mine, mine, l_send.at[i], l_recv.at[i], x_peer(dx)[1]) for i, dx in enumerate(WAYS)]
+    for c in range(INIT, CHUNKS):
+        send_grads(c)
+
+    @pl.when(core == 1)
+    def _():
+        for dz in range(1, NZ):
+            pl.semaphore_signal(barrier, inc=1, device_id=z_peer(dz)[1], device_id_type=MESH)
+        for dy in range(1, NYH):
+            peer = ((lax.rem(yh + dy, NYH) * NZ + z) * NC + core, me)
+            pl.semaphore_signal(barrier, inc=1, device_id=peer, device_id_type=MESH)
+
+    loads[2].wait()
+    for j in range(n_blocks):
+        global_rows[:, j, :] = global_v[:, j * BLOCK : (j + 1) * BLOCK]
+    loads[3].wait()
+    delta = global_rows[...].reshape(n_rows, BLOCK) - local_v[...]
+    scale = (jnp.max(jnp.abs(delta), axis=1, keepdims=True) + EPS).astype(jnp.bfloat16).astype(jnp.float32)
+    codes = (delta / scale).astype(jnp.bfloat16)
+    values[...] = (codes.astype(jnp.float32) * scale).astype(jnp.bfloat16)
+
+    a1, a2, a3 = [], [], []
+    mean_rows = average.at[ds(z * rz, rz), :]
+    for dz in range(1, NZ):
+        pz, device = z_peer(dz)
+        a1.append(remote(values.at[ds(pz * rz, rz), :], part1.at[z], a1_send.at[dz], a1_recv.at[dz], device))
+        a3.append(remote(mean_rows, mean_rows, a3_send.at[dz], a3_recv.at[dz], device))
+    for k in range(1, group):
+        a2.append(remote(part2.at[g_me], part2.at[g_me], a2_send.at[k], a2_recv.at[k], g_peer(k)[1]))
+
+    def meet_far():
+        @pl.when(core == 1)
+        def _():
+            pl.semaphore_wait(barrier, NZ - 1 + NYH - 1)
+            pl.semaphore_signal(far_sem, inc=1, device_id=(first, me), device_id_type=MESH)
+
+        @pl.when(core == 0)
+        def _():
+            pl.semaphore_wait(far_sem, 1)
+
+        for copy in a1:
+            copy.start()
 
     def reduce_z():
         part1[z] = values[ds(z * rz, rz), :]
         for copy in a1:
             copy.wait_recv()
         part2[g_me] = jnp.sum(part1[...].astype(jnp.float32), axis=0)
-        return [
-            send(part2.at[g_me], part2.at[g_me], a2_send.at[k], a2_recv.at[k], g_peer(k)[1]) for k in range(1, group)
-        ]
-
-    def reduce_group(a2):
+        for copy in a2:
+            copy.start()
+
+    def reduce_group():
         for copy in a2:
             copy.wait_recv()
-        mine = average.at[ds(z * rz, rz), :]
-        mine[...] = jnp.sum(part2[...], axis=0) / float(NZ * group)
-        return [send(mine, mine, a3_send.at[dz], a3_recv.at[dz], z_peer(dz)[1]) for dz in range(1, NZ)]
-
-    def outer_update(a3):
+        mean_rows[...] = jnp.sum(part2[...], axis=0) / float(NZ * group)
+        for copy in a3:
+            copy.start()
+
+    def outer_update():
         for copy in a3:
             copy.wait_recv()
         loads[4].wait()
@@ -200,15 +243,16 @@
         store.start()
         stores.append(store)
 
-    a2 = reduce_z()
-    a3 = None
+    steps = (meet_far, reduce_z, reduce_group)
+    early = z < EARLY_Z
     for c in range(CHUNKS):
+        for at, wanted in ((EARLY_STEPS, early), (LATE_STEPS, jnp.logical_not(early))):
+            if c in at:
+                pl.when(wanted)(steps[at.index(c)])
         multiply(c)
-        if c == 0:
-            a3 = reduce_group(a2)
-        else:
+        if c:
             finish(c - 1)
-    outer_update(a3)
+    outer_update()
     finish(CHUNKS - 1)
 
     for copy in outs:
@@ -217,6 +261,22 @@
         copy.wait()
     for copy in sends:
         copy.wait_send()
+
+
+def hand_over(*refs):
+    ins, outs, held, (in_sem, out_sem) = refs[:3], refs[3:6], refs[6:9], refs[9:]
+    quarter = ins[2].shape[1] // 4
+    views = [lambda ref, i=i: ref.at[:, pl.ds(i * quarter, quarter), :] for i in range(4)]
+    moves = [(2, view) for view in views] + [(0, lambda ref: ref), (1, lambda ref: ref)]
+    loads = [pltpu.make_async_copy(view(ins[k]), view(held[k]), in_sem.at[i]) for i, (k, view) in enumerate(moves)]
+    stores = [pltpu.make_async_copy(view(held[k]), view(outs[k]), out_sem.at[i]) for i, (k, view) in enumerate(moves)]
+    for copy in loads:
+        copy.start()
+    for load, store in zip(loads, stores):
+        load.wait()
+        store.start()
+    for copy in stores:
+        copy.wait()
 
 
 def local(dims, local_params, global_params, momentum, layer_input, output_grad, token_ids):
@@ -238,7 +298,7 @@
             jax.ShapeDtypeStruct((rows, d), bf16),
         ),
         in_specs=[anywhere] * 6,
-        out_specs=(vmem, vmem, anywhere),
+        out_specs=(vmem, vmem, vmem),
         scratch_shapes=[
             pltpu.VMEM((n_rows, BLOCK), f32),
             pltpu.VMEM((frag, d), f32),
@@ -257,7 +317,8 @@
             pltpu.VMEM((2, half, w), f32),
             pltpu.VMEM((CHUNKS, half, w), bf16),
             dma((5,)), dma(()), dma((CHUNKS,)),
-            dma((NX,)), dma((NX,)),
+            pltpu.SemaphoreType.REGULAR, pltpu.SemaphoreType.REGULAR,
+            dma((NX - 1,)), dma((NX - 1,)),
             dma((CHUNKS, NX)), dma((CHUNKS, NX)),
             dma((CHUNKS,)), dma((CHUNKS,)),
             dma((CHUNKS, NX)), dma((CHUNKS, NX)),
@@ -266,7 +327,7 @@
             dma((nz,)), dma((nz,)),
         ],
         compiler_params=pltpu.CompilerParams(
-            collective_id=0, has_side_effects=True, vmem_limit_bytes=32 * 1024 * 1024
+            collective_id=0, has_side_effects=True, vmem_limit_bytes=60 * 1024 * 1024
         ),
     )(
         local_params.reshape(n_rows, BLOCK),
@@ -276,7 +337,18 @@
         output_grad[0],
         token_ids,
     )
-    return new_global, new_momentum, inner_grad[None]
+    return pl.pallas_call(
+        hand_over,
+        out_shape=(
+            jax.ShapeDtypeStruct((frag, d), f32),
+            jax.ShapeDtypeStruct((frag, d), f32),
+            jax.ShapeDtypeStruct((1, rows, d), bf16),
+        ),
+        in_specs=[anywhere] * 3,
+        out_specs=(anywhere,) * 3,
+        scratch_shapes=[pltpu.VMEM((frag, d), f32), pltpu.VMEM((frag, d), f32), pltpu.VMEM((1, rows, d), bf16), dma((6,)), dma((6,))],
+        compiler_params=pltpu.CompilerParams(vmem_limit_bytes=60 * 1024 * 1024),
+    )(new_global, new_momentum, inner_grad[None])
 
 
 def build(mesh, dims):

time: 70 us -> 61 us (0.87)
  local copies, waits for them, and re-layouts: 8.34 us -> 0 us
    unnamed x15 -> x0, local copies, waits for them, and re-layouts: 8.34 us -> none
    pallas_call x1, Pallas kernels: 60.3 us -> 58 us  [local(): pl.pallas_call(functools.partial(kernel, dims), out_shape=(jax.ShapeDtype...]
    pallas_call x0 -> x1, Pallas kernels: none -> 2.19 us  [local(): pl.pallas_call(hand_over, out_shape=(jax.ShapeDtypeStruct((frag, d), f32)...]
where the time goes in v2:
time: 61 us; the launch traced here: 60.8 us
  Pallas kernels  60.2 us (99%)
  between operations  0.64 us (1%)
    pallas_call x1, Pallas kernels, local(): pl.pallas_call(functools.partial(kernel, dims), out_shape=(jax.ShapeDtype...  58 us
    pallas_call x1, Pallas kernels, local(): pl.pallas_call(hand_over, out_shape=(jax.ShapeDtypeStruct((frag, d), f32)...  2.19 us

profile of v2, /device:TPU:1, one launch (start us, length us, event | category | flops | bytes accessed | tf_op | source)
XLA Modules:
  0.0 60.8 jit_solution(729314676858541538)
XLA Ops:
  0.6 58.0 %shard_map.85 = (f32[6,8192]{1,0:T(8,128)}, f32[6,8192]{1,0:T(8,128)}, bf16[64,8192]{1,0:T(8,128)(2,1)}) custom-call(f32[384,128]{1,0:T(8,128)} %bitcast.6, f32[6,8192]{1,0:T(8,128)} %global_hbm.1, f32[6,8192]{1,0:T(8,128)} %momentum_hbm.1, bf16[128,512]{1,0:T(8,128)(2,1)} %bitcast.7, bf16[128,8192]{1,0:T(8,128)(2,1)} %bitcast.4, s32[1,128]{1,0:T(1,128)} %ids_hbm.1), custom_call_target="tpu_custom_call" | custom-call | tf_op jit(solution)/shard_map/pallas_call | solution.py:293
  58.6 2.2 %shard_map.86 = (f32[6,8192]{1,0:T(8,128)}, f32[6,8192]{1,0:T(8,128)}, bf16[1,64,8192]{2,1,0:T(8,128)(2,1)}) custom-call(f32[6,8192]{1,0:T(8,128)} %get-tuple-element.6.refs_0_, f32[6,8192]{1,0:T(8,128)} %get-tuple-element.7.refs_1_, bf16[1,64,8192]{2,1,0:T(8,128)(2,1)} %bitcast.5), custom_call_target="tpu_custom_call" | custom-call | tf_op jit(solution)/shard_map/pallas_call | solution.py:340

commit v3 on v2

--- a/solution.py
+++ b/solution.py
@@ -15,11 +15,14 @@
 BLOCK = 128
 NX = 4
 NY = 2
-CHUNKS = 8
+WIDTHS = (256,) * 8
+CHUNKS = len(WIDTHS)
+STARTS = tuple(sum(WIDTHS[:c]) for c in range(CHUNKS))
+AHEAD = 8
 INIT = 1
 WAYS = (2, 1, 3)
 EARLY_Z = 5
-EARLY_STEPS, LATE_STEPS = (1, 3, 4), (0, 1, 2)
+EARLY_STEPS, LATE_STEPS = (1, 4, 5), (0, 2, 4)
 
 
 def ds(start, size):
@@ -50,7 +53,6 @@
     rows = r_in // (NX * NY)
     half = r_in // NY
     cols = d // NX
-    w = cols // CHUNKS
     n_blocks = d // BLOCK
     frag = global_v.shape[0]
     n_rows = local_v.shape[0]
@@ -87,21 +89,18 @@
     own_grads.start()
 
     barrier = pltpu.get_barrier_semaphore()
-    first, second = replica - core, replica - core + 1
-    near = [lax.rem(x + dx, NX) * NY + y for dx in range(1, NX)] + [x * NY + (1 - y)]
-    for peer in near:
-        pl.semaphore_signal(barrier, inc=1, device_id=(first, peer), device_id_type=MESH)
-
-    @pl.when(core == 1)
+    for px in range(NX):
+
+        @pl.when(jnp.logical_or(y == 0, x != px))
+        def _():
+            pl.semaphore_signal(barrier, inc=1, device_id=(replica, px * NY + 1), device_id_type=MESH)
+
+    @pl.when(y == 1)
     def _():
-        pl.semaphore_signal(barrier, inc=1, device_id=(first, me), device_id_type=MESH)
-
-    @pl.when(core == 0)
-    def _():
-        pl.semaphore_wait(barrier, NC * len(near) + 1)
-        pl.semaphore_signal(go_sem, inc=1, device_id=(second, me), device_id_type=MESH)
-
-    @pl.when(core == 1)
+        pl.semaphore_wait(barrier, NX * NY - 1)
+        pl.semaphore_signal(go_sem, inc=1, device_id=y_peer, device_id_type=MESH)
+
+    @pl.when(y == 0)
     def _():
         pl.semaphore_wait(go_sem, 1)
 
@@ -119,6 +118,12 @@
         copy.start()
         return copy
 
+    def span(c):
+        return slice(STARTS[c], STARTS[c] + WIDTHS[c])
+
+    def column(px, c):
+        return pl.ds(pl.multiple_of(px * cols + STARTS[c], BLOCK), WIDTHS[c])
+
     gs = [[] for _ in range(CHUNKS)]
 
     def send_grads(c):
@@ -126,8 +131,8 @@
             px, device = x_peer(dx)
             gs[c].append(
                 send(
-                    grad_hbm.at[:, ds(px * cols + c * w, w)],
-                    grads.at[ds(x * tokens, tokens), c * w : (c + 1) * w],
+                    grad_hbm.at[:, column(px, c)],
+                    grads.at[ds(x * tokens, tokens), span(c)],
                     g_send.at[c, dx], g_recv.at[c, dx], device,
                 )
             )
@@ -146,15 +151,12 @@
 
     mine = inputs_t.at[:, :, ds(x * tokens, tokens)]
     ls = [send(mine, mine, l_send.at[i], l_recv.at[i], x_peer(dx)[1]) for i, dx in enumerate(WAYS)]
-    for c in range(INIT, CHUNKS):
+    for c in range(INIT, AHEAD):
         send_grads(c)
 
-    @pl.when(core == 1)
+    @pl.when(y == 0)
     def _():
-        for dz in range(1, NZ):
-            pl.semaphore_signal(barrier, inc=1, device_id=z_peer(dz)[1], device_id_type=MESH)
-        for dy in range(1, NYH):
-            peer = ((lax.rem(yh + dy, NYH) * NZ + z) * NC + core, me)
+        for peer in [z_peer(dz)[1] for dz in range(1, NZ)] + [g_peer(k)[1] for k in range(1, group)]:
             pl.semaphore_signal(barrier, inc=1, device_id=peer, device_id_type=MESH)
 
     loads[2].wait()
@@ -176,12 +178,12 @@
         a2.append(remote(part2.at[g_me], part2.at[g_me], a2_send.at[k], a2_recv.at[k], g_peer(k)[1]))
 
     def meet_far():
-        @pl.when(core == 1)
+        @pl.when(y == 0)
         def _():
-            pl.semaphore_wait(barrier, NZ - 1 + NYH - 1)
-            pl.semaphore_signal(far_sem, inc=1, device_id=(first, me), device_id_type=MESH)
-
-        @pl.when(core == 0)
+            pl.semaphore_wait(barrier, NZ - 1 + group - 1)
+            pl.semaphore_signal(far_sem, inc=1, device_id=y_peer, device_id_type=MESH)
+
+        @pl.when(y == 1)
         def _():
             pl.semaphore_wait(far_sem, 1)
 
@@ -218,28 +220,30 @@
     ys, outs = [], []
 
     def multiply(c):
-        at = slice(c * w, (c + 1) * w)
+        at = span(c)
         if c == 0:
             own_grads.wait()
             for copy in ls:
                 copy.wait_recv()
         for copy in gs[c]:
             copy.wait_recv()
+        if c + AHEAD < CHUNKS:
+            send_grads(c + AHEAD)
         block = grads[:, at]
-        y_out[c] = jnp.dot(inputs_t[1 - y], block, preferred_element_type=jnp.float32).astype(jnp.bfloat16)
-        ys.append(send(y_out.at[c], y_in.at[c], y_send.at[c], y_recv.at[c], y_peer))
-        own_half[c % 2] = jnp.dot(inputs_t[y], block, preferred_element_type=jnp.float32)
+        y_out[:, at] = jnp.dot(inputs_t[1 - y], block, preferred_element_type=jnp.float32).astype(jnp.bfloat16)
+        ys.append(send(y_out.at[:, at], y_in.at[:, at], y_send.at[c], y_recv.at[c], y_peer))
+        own_half[c % 2, :, : WIDTHS[c]] = jnp.dot(inputs_t[y], block, preferred_element_type=jnp.float32)
 
     stores = []
 
     def finish(c):
         ys[c].wait_recv()
-        done[c] = (own_half[c % 2] + y_in[c].astype(jnp.float32)).astype(jnp.bfloat16)
-        to = ds(x * cols + c * w, w)
+        at, to = span(c), column(x, c)
+        done[:, at] = (own_half[c % 2, :, : WIDTHS[c]] + y_in[:, at].astype(jnp.float32)).astype(jnp.bfloat16)
         for dx in range(1, NX):
             px, device = x_peer(dx)
-            outs.append(send(done.at[c, ds(px * rows, rows), :], out_ref.at[:, to], o_send.at[c, dx], o_recv.at[c, dx], device))
-        store = pltpu.make_async_copy(done.at[c, ds(x * rows, rows), :], out_ref.at[:, to], store_sem.at[c])
+            outs.append(send(done.at[ds(px * rows, rows), at], out_ref.at[:, to], o_send.at[c, dx], o_recv.at[c, dx], device))
+        store = pltpu.make_async_copy(done.at[ds(x * rows, rows), at], out_ref.at[:, to], store_sem.at[c])
         store.start()
         stores.append(store)
 
@@ -247,13 +251,14 @@
     early = z < EARLY_Z
     for c in range(CHUNKS):
         for at, wanted in ((EARLY_STEPS, early), (LATE_STEPS, jnp.logical_not(early))):
-            if c in at:
-                pl.when(wanted)(steps[at.index(c)])
+            for step, before in zip(steps, at):
+                if before == c:
+                    pl.when(wanted)(step)
         multiply(c)
         if c:
             finish(c - 1)
+    finish(CHUNKS - 1)
     outer_update()
-    finish(CHUNKS - 1)
 
     for copy in outs:
         copy.wait_recv()
@@ -285,7 +290,6 @@
     n_rows = frag * d // BLOCK
     nz, group = dims[1], dims[0] * dims[2]
     half, cols, rows = r_in // NY, d // NX, r_in // (NX * NY)
-    w = cols // CHUNKS
     f32, bf16 = jnp.float32, jnp.bfloat16
     dma = pltpu.SemaphoreType.DMA
     anywhere = pl.BlockSpec(memory_space=pl.ANY)
@@ -312,10 +316,10 @@
             pltpu.VMEM((n_rows, BLOCK), f32),
             pltpu.VMEM((NY, half, NX * tokens), bf16),
             pltpu.VMEM((NX * tokens, cols), bf16),
-            pltpu.VMEM((CHUNKS, half, w), bf16),
-            pltpu.VMEM((CHUNKS, half, w), bf16),
-            pltpu.VMEM((2, half, w), f32),
-            pltpu.VMEM((CHUNKS, half, w), bf16),
+            pltpu.VMEM((half, cols), bf16),
+            pltpu.VMEM((half, cols), bf16),
+            pltpu.VMEM((2, half, max(WIDTHS)), f32),
+            pltpu.VMEM((half, cols), bf16),
             dma((5,)), dma(()), dma((CHUNKS,)),
             pltpu.SemaphoreType.REGULAR, pltpu.SemaphoreType.REGULAR,
             dma((NX - 1,)), dma((NX - 1,)),

time: 61 us -> 59.2 us (0.970)
  Pallas kernels: 60.2 us -> 58 us
    pallas_call x1, Pallas kernels: 58 us -> 55.9 us  [local(): pl.pallas_call(functools.partial(kernel, dims), out_shape=(jax.ShapeDtype...]
where the time goes in v3:
time: 59.2 us; the launch traced here: 58.7 us
  Pallas kernels  58 us (98%)
  between operations  0.64 us (1%)
    pallas_call x1, Pallas kernels, local(): pl.pallas_call(functools.partial(kernel, dims), out_shape=(jax.ShapeDtype...  55.9 us
    pallas_call x1, Pallas kernels, local(): pl.pallas_call(hand_over, out_shape=(jax.ShapeDtypeStruct((frag, d), f32)...  2.19 us

profile of v3, /device:TPU:1, one launch (start us, length us, event | category | flops | bytes accessed | tf_op | source)
XLA Modules:
  0.0 58.7 jit_solution(7347125502871902423)
XLA Ops:
  0.6 55.9 %shard_map.85 = (f32[6,8192]{1,0:T(8,128)}, f32[6,8192]{1,0:T(8,128)}, bf16[64,8192]{1,0:T(8,128)(2,1)}) custom-call(f32[384,128]{1,0:T(8,128)} %bitcast.6, f32[6,8192]{1,0:T(8,128)} %global_hbm.1, f32[6,8192]{1,0:T(8,128)} %momentum_hbm.1, bf16[128,512]{1,0:T(8,128)(2,1)} %bitcast.7, bf16[128,8192]{1,0:T(8,128)(2,1)} %bitcast.4, s32[1,128]{1,0:T(1,128)} %ids_hbm.1), custom_call_target="tpu_custom_call" | custom-call | tf_op jit(solution)/shard_map/pallas_call | solution.py:297
  56.5 2.2 %shard_map.86 = (f32[6,8192]{1,0:T(8,128)}, f32[6,8192]{1,0:T(8,128)}, bf16[1,64,8192]{2,1,0:T(8,128)(2,1)}) custom-call(f32[6,8192]{1,0:T(8,128)} %get-tuple-element.6.refs_0_, f32[6,8192]{1,0:T(8,128)} %get-tuple-element.7.refs_1_, bf16[1,64,8192]{2,1,0:T(8,128)(2,1)} %bitcast.5), custom_call_target="tpu_custom_call" | custom-call | tf_op jit(solution)/shard_map/pallas_call | solution.py:344

commit v4 on v3

--- a/solution.py
+++ b/solution.py
@@ -22,7 +22,7 @@
 INIT = 1
 WAYS = (2, 1, 3)
 EARLY_Z = 5
-EARLY_STEPS, LATE_STEPS = (1, 4, 5), (0, 2, 4)
+EARLY_STEPS, LATE_STEPS = (1, 4, 6), (0, 2, 4)
 
 
 def ds(start, size):

time: 59.2 us -> 59.8 us (1.010); the launches traced: 58.7 us -> 58.7 us
  no operation moved by 1% of the time
where the time goes in v4:
time: 59.8 us; the launch traced here: 58.7 us
  Pallas kernels  58 us (97%)
  between operations  0.64 us (1%)
    pallas_call x1, Pallas kernels, local(): pl.pallas_call(functools.partial(kernel, dims), out_shape=(jax.ShapeDtype...  55.9 us
    pallas_call x1, Pallas kernels, local(): pl.pallas_call(hand_over, out_shape=(jax.ShapeDtypeStruct((frag, d), f32)...  2.19 us

profile of v4, /device:TPU:1, one launch (start us, length us, event | category | flops | bytes accessed | tf_op | source)
XLA Modules:
  0.0 58.7 jit_solution(11254215787968598840)
XLA Ops:
  0.6 55.9 %shard_map.85 = (f32[6,8192]{1,0:T(8,128)}, f32[6,8192]{1,0:T(8,128)}, bf16[64,8192]{1,0:T(8,128)(2,1)}) custom-call(f32[384,128]{1,0:T(8,128)} %bitcast.6, f32[6,8192]{1,0:T(8,128)} %global_hbm.1, f32[6,8192]{1,0:T(8,128)} %momentum_hbm.1, bf16[128,512]{1,0:T(8,128)(2,1)} %bitcast.7, bf16[128,8192]{1,0:T(8,128)(2,1)} %bitcast.4, s32[1,128]{1,0:T(1,128)} %ids_hbm.1), custom_call_target="tpu_custom_call" | custom-call | tf_op jit(solution)/shard_map/pallas_call | solution.py:297
  56.5 2.2 %shard_map.86 = (f32[6,8192]{1,0:T(8,128)}, f32[6,8192]{1,0:T(8,128)}, bf16[1,64,8192]{2,1,0:T(8,128)(2,1)}) custom-call(f32[6,8192]{1,0:T(8,128)} %get-tuple-element.6.refs_0_, f32[6,8192]{1,0:T(8,128)} %get-tuple-element.7.refs_1_, bf16[1,64,8192]{2,1,0:T(8,128)(2,1)} %bitcast.5), custom_call_target="tpu_custom_call" | custom-call | tf_op jit(solution)/shard_map/pallas_call | solution.py:344
